TPU v7x, 512 devices: a whole 4x4x16 slice. The times are simulated.
512 devices in a mesh: wide: 128 (over z, y, core), narrow: 4 (over x).
Axes of the slice: x: 4, y: 4, z: 16, core: 2. Of those that a mesh axis runs over, the one named last changes fastest.
Arguments:
- coefficients: bfloat16 [100, 2097152], P(None, ('wide', 'narrow')), may hold values from -6 to 6
- neighbours: int32 [4, 2097152], P(None, ('wide', 'narrow')), may hold values from 0 to 5119
- halo_blocks: int32 [512, 4, 2], P(('wide', 'narrow')), may hold values from 0 to 31, as said below
- recon_weight: bfloat16 [5, 75, 100], replicated, may hold values from -0.25 to 0.25
- owner_device: int32 [16384], P(('wide', 'narrow')), may hold values from 0 to 511, as said below
- work_count: int32 [16384], P(('wide', 'narrow')), may hold values from 1 to 4
Outputs:
- migrated_modal: bfloat16 [100, 2097152], P(None, ('wide', 'narrow'))
- migrated_metric: float32 [6, 2097152], P(None, ('wide', 'narrow'))
- migrated_work: float32 [2097152], P(('wide', 'narrow'))
Inputs may be any that keep to these rules, and one draw needn't show every extreme that they name: `halo_blocks`: each device's list for one direction holds 2 different block numbers of that device. `owner_device`: every device receives exactly 32 blocks. Of one device's blocks, either exactly 1 or none go to devices of any one wide index. Two devices of the same wide index with narrow indices 2j and 2j + 1 together send either exactly 1 or none of their blocks to devices of any one wide index. For every wide index w and narrow indices a and c, exactly 8 of the blocks that devices of narrow index a send to wide index w go to the device of wide index w and narrow index c.
All inputs are finite; a program needn't handle non-finite values.
Results may differ from a plain program's by a relative error of at most 0.0004.
Values may be sent and summed in bfloat16 or wider, within the bound.
A program may use at most 64 MiB of HBM per device.

v0:
```python
import jax
import jax.numpy as jnp
from jax import lax
from jax.sharding import PartitionSpec as P


def passed_along(value, axis, steps):
    count = lax.axis_size(axis)
    pairs = [(source, (source + steps) % count) for source in range(count)]
    return lax.ppermute(value, axis, pairs)


def swapped(value, axis, apart):
    return lax.ppermute(value, axis, [(i, i ^ 1 << apart) for i in range(lax.axis_size(axis))])


def metric_rows(derivs):
    vectors = derivs.reshape(derivs.shape[0] // 3, 3, derivs.shape[1])
    inverse = 1.0 / vectors.shape[0]
    along_x = vectors[:, 0]
    along_y = vectors[:, 1]
    along_z = vectors[:, 2]
    return jnp.stack(
        [
            1.0 + inverse * jnp.sum(along_x * along_x, axis=0),
            1.0 + inverse * jnp.sum(along_y * along_y, axis=0),
            1.0 + inverse * jnp.sum(along_z * along_z, axis=0),
            inverse * jnp.sum(along_x * along_y, axis=0),
            inverse * jnp.sum(along_x * along_z, axis=0),
            inverse * jnp.sum(along_y * along_z, axis=0),
        ]
    )


def determinant(components):
    metric_xx = components[0]
    metric_yy = components[1]
    metric_zz = components[2]
    metric_xy = components[3]
    metric_xz = components[4]
    metric_yz = components[5]
    return (
        metric_xx * (metric_yy * metric_zz - metric_yz * metric_yz)
        - metric_xy * (metric_xy * metric_zz - metric_yz * metric_xz)
        + metric_xz * (metric_xy * metric_yz - metric_yy * metric_xz)
    )


def first_slots(slot_of, slot_total, position):
    slot_ids = jnp.arange(slot_total, dtype=jnp.int32)
    matches = slot_of[None, :] == slot_ids[:, None]
    filled = jnp.any(matches, axis=1)
    picked = jnp.sum(jnp.where(matches, position[None, :], 0), axis=1)
    return (filled, picked)


def per_device(coefficients, neighbours, halo_blocks, recon_weight, owner_device, work_count):
    coeff_count, elem_count = coefficients.shape
    block_count = owner_device.shape[0]
    block_len = elem_count // block_count
    halo_count = halo_blocks.shape[2]
    wide_size = lax.axis_size("wide")
    narrow_size = lax.axis_size("narrow")
    blocked = coefficients.reshape(coeff_count, block_count, block_len)
    sending = halo_blocks[0]

    def outgoing(direction):
        return jnp.take(blocked, sending[direction], axis=1)

    def from_wide(block_set, offset):
        return passed_along(block_set, "wide", offset)

    def from_narrow(block_set, offset):
        return passed_along(block_set, "narrow", offset)

    arrived = [
        from_wide(outgoing(1), 1),
        from_wide(outgoing(0), -1),
        from_narrow(outgoing(3), 1),
        from_narrow(outgoing(2), -1),
    ]
    halo_cols = jnp.concatenate(arrived, axis=1).reshape(coeff_count, 4 * halo_count * block_len)
    derivs = jnp.dot(recon_weight[0], coefficients, preferred_element_type=jnp.float32)
    extended = jnp.concatenate([coefficients, halo_cols], axis=1)
    for face_index in range(4):
        gathered = jnp.take(extended, neighbours[face_index], axis=1)
        derivs = derivs + jnp.dot(
            recon_weight[face_index + 1], gathered, preferred_element_type=jnp.float32
        )
    components = metric_rows(derivs)
    work_est = jnp.repeat(work_count.astype(jnp.float32), block_len) * jnp.sqrt(
        determinant(components)
    )
    components, work_est = lax.optimization_barrier((components, work_est))
    stats = jnp.concatenate([components, work_est[None, :]], axis=0).reshape(
        7, block_count, block_len
    )
    wide_target = owner_device // narrow_size
    narrow_target = owner_device % narrow_size
    position = jnp.arange(block_count, dtype=jnp.int32)
    earlier = (wide_target[None, :] == wide_target[:, None]) & (
        position[None, :] < position[:, None]
    )
    rank_of = jnp.sum(earlier.astype(jnp.int32), axis=1)
    member = lax.axis_index("narrow") % 2
    other = 1 - member
    half_len = block_len // 2
    pair_wide = max(1, 2 * block_count // wide_size)
    pair_total = wide_size * pair_wide
    pair_ids = jnp.arange(pair_total, dtype=jnp.int32)
    pair_slot = wide_target * pair_wide + rank_of
    own_coeffs = lax.dynamic_slice_in_dim(blocked, member * half_len, half_len, 2)
    own_stats = lax.dynamic_slice_in_dim(stats, member * half_len, half_len, 2)
    give_coeffs = lax.dynamic_slice_in_dim(blocked, other * half_len, half_len, 2)
    give_stats = lax.dynamic_slice_in_dim(stats, other * half_len, half_len, 2)
    labels = jnp.stack([pair_slot, narrow_target]).astype(jnp.float32)
    partner_coeffs = swapped(give_coeffs, "narrow", 0)
    partner_stats, partner_labels = swapped((give_stats, labels), "narrow", 0)
    partner_slot = partner_labels[0].astype(jnp.int32)
    partner_target = partner_labels[1].astype(jnp.int32)
    own_has, own_pick = first_slots(pair_slot, pair_total, position)
    partner_has, partner_pick = first_slots(partner_slot, pair_total, position)
    zero_coeff = jnp.zeros((), blocked.dtype)
    joined_coeffs = jnp.where(
        own_has[None, :, None],
        jnp.take(own_coeffs, own_pick, axis=1),
        jnp.where(
            partner_has[None, :, None], jnp.take(partner_coeffs, partner_pick, axis=1), zero_coeff
        ),
    )
    joined_stats = jnp.where(
        own_has[None, :, None],
        jnp.take(own_stats, own_pick, axis=1),
        jnp.where(partner_has[None, :, None], jnp.take(partner_stats, partner_pick, axis=1), 0.0),
    )
    pair_tags = jnp.where(
        own_has,
        jnp.take(narrow_target, own_pick) * 2 + member,
        jnp.where(partner_has, jnp.take(partner_target, partner_pick) * 2 + other, -1),
    )
    stats_in, tags_in = (
        lax.all_to_all(joined_stats, "wide", split_axis=1, concat_axis=1, tiled=True),
        lax.all_to_all(
            pair_tags.astype(jnp.float32)[None, :], "wide", split_axis=1, concat_axis=1, tiled=True
        ),
    )
    coeffs_in = lax.all_to_all(joined_coeffs, "wide", split_axis=1, concat_axis=1, tiled=True)
    arrived_tags = tags_in[0].astype(jnp.int32)
    anchor = jnp.where(arrived_tags >= 0, arrived_tags % 2, -1)
    keep_order = jnp.argsort(jnp.where(anchor == member, 0, 1) * pair_total + pair_ids)[
        :block_count
    ]
    pass_order = jnp.argsort(jnp.where(anchor == other, 0, 1) * pair_total + pair_ids)[:block_count]
    returned_coeffs = swapped(jnp.take(coeffs_in, pass_order, axis=1), "narrow", 0)
    returned_stats = swapped(jnp.take(stats_in, pass_order, axis=1), "narrow", 0)
    kept_coeffs = jnp.take(coeffs_in, keep_order, axis=1)
    kept_stats = jnp.take(stats_in, keep_order, axis=1)
    at_front = member == 0
    whole_coeffs = jnp.concatenate(
        [
            jnp.where(at_front, kept_coeffs, returned_coeffs),
            jnp.where(at_front, returned_coeffs, kept_coeffs),
        ],
        axis=2,
    )
    whole_stats = jnp.concatenate(
        [
            jnp.where(at_front, kept_stats, returned_stats),
            jnp.where(at_front, returned_stats, kept_stats),
        ],
        axis=2,
    )
    through = jnp.argsort(jnp.take(arrived_tags, keep_order) // 2 * block_count + position)
    relayed_coeffs = jnp.take(whole_coeffs, through, axis=1)
    relayed_stats = jnp.take(whole_stats, through, axis=1)
    new_coeffs = lax.all_to_all(relayed_coeffs, "narrow", split_axis=1, concat_axis=1, tiled=True)
    new_stats = lax.all_to_all(relayed_stats, "narrow", split_axis=1, concat_axis=1, tiled=True)
    flat_stats = new_stats.reshape(7, elem_count)
    return (new_coeffs.reshape(coeff_count, elem_count), flat_stats[:6], flat_stats[6])


def solution(mesh):
    return jax.shard_map(
        per_device,
        mesh=mesh,
        in_specs=(
            P(None, ("wide", "narrow")),
            P(None, ("wide", "narrow")),
            P(("wide", "narrow"), None, None),
            P(),
            P(("wide", "narrow")),
            P(("wide", "narrow")),
        ),
        out_specs=(P(None, ("wide", "narrow")), P(None, ("wide", "narrow")), P(("wide", "narrow"))),
        check_vma=False,
    )
```

profile of v0, /device:TPU:32, one launch (start us, length us, event | category | flops | bytes accessed | tf_op | source)
XLA Modules:
  0.0 322.5 jit_solution(11149431525572227855)
XLA Ops:
  1.7 1.6 copy.50
  4.7 2.0 collective-permute-start.3
  7.4 5.7 %collective-permute-start.4 = (bf16[100,2,128]{2,0,1:T(8,128)(2,1)S(1)}, bf16[100,2,128]{2,0,1:T(8,128)(2,1)S(1)}, u32[]{:S(2)}, u32[]{:S(2)}) collective-permute-start(bf16[100,2,128]{2,0,1:T(8,128)(2,1)S(1)} %select_bitcast_fusion.6), channel_id=1, source_target_pairs={{0,508},{4,0},{8,4},{12,8},{16,12},{20,16},{24,20},{28,24},{32,28}... | collective-permute-start | bytes 153608 | tf_op jit(solution)/shard_map/ppermute | solution.py:10
  13.9 3.4 %collective-permute-start.5 = (bf16[100,2,128]{2,0,1:T(8,128)(2,1)S(1)}, bf16[100,2,128]{2,0,1:T(8,128)(2,1)S(1)}, u32[]{:S(2)}, u32[]{:S(2)}) collective-permute-start(bf16[100,2,128]{2,0,1:T(8,128)(2,1)S(1)} %select_bitcast_fusion.5), channel_id=1, source_target_pairs={{0,1},{1,2},{2,3},{3,0},{4,5},{5,6},{6,7},{7,4},{8,9},{9,10},{10,1... | collective-permute-start | bytes 153608 | tf_op jit(solution)/shard_map/ppermute | solution.py:10
  17.9 3.6 %collective-permute-start.6 = (bf16[100,2,128]{2,0,1:T(8,128)(2,1)S(1)}, bf16[100,2,128]{2,0,1:T(8,128)(2,1)S(1)}, u32[]{:S(2)}, u32[]{:S(2)}) collective-permute-start(bf16[100,2,128]{2,0,1:T(8,128)(2,1)S(1)} %select_bitcast_fusion.4), channel_id=1, source_target_pairs={{0,3},{1,0},{2,1},{3,2},{4,7},{5,4},{6,5},{7,6},{8,11},{9,8},{10,9... | collective-permute-start | bytes 153608 | tf_op jit(solution)/shard_map/ppermute | solution.py:10
  21.8 2.2 collective-permute-start
  30.8 14.9 %gather_fusion.13 = bf16[4096,100]{1,0:T(8,128)(2,1)} fusion(bf16[100,5120]{0,1:T(8,128)(2,1)S(1)} %pad_maximum_fusion, s32[4096]{0:T(1024)S(1)} %fusion.38), kind=kCustom, calls=%fused_computation.4.clone | custom fusion | bytes 1654784 | tf_op jit(solution)/shard_map/jit(_take)/gather | solution.py:86
  45.7 14.9 %gather_fusion.14 = bf16[4096,100]{1,0:T(8,128)(2,1)} fusion(bf16[100,5120]{0,1:T(8,128)(2,1)S(1)} %pad_maximum_fusion, s32[4096]{0:T(1024)S(1)} %fusion.39), kind=kCustom, calls=%fused_computation.13.clone | custom fusion | bytes 1654784 | tf_op jit(solution)/shard_map/jit(_take)/gather | solution.py:86
  60.6 14.9 %gather_fusion.15 = bf16[4096,100]{1,0:T(8,128)(2,1)} fusion(bf16[100,5120]{0,1:T(8,128)(2,1)S(1)} %pad_maximum_fusion, s32[4096]{0:T(1024)S(1)} %fusion.40), kind=kCustom, calls=%fused_computation.14.clone | custom fusion | bytes 1654784 | tf_op jit(solution)/shard_map/jit(_take)/gather | solution.py:86
  75.4 12.1 %gather_fusion.16 = bf16[4096,100]{1,0:T(8,128)(2,1)S(1)} fusion(bf16[100,5120]{0,1:T(8,128)(2,1)S(1)} %pad_maximum_fusion, s32[4096]{0:T(1024)S(1)} %fusion.41), kind=kCustom, calls=%fused_computation.15.clone | custom fusion | bytes 1654784 | tf_op jit(solution)/shard_map/jit(_take)/gather | solution.py:86
  87.6 2.5 fusion.3
  93.0 1.7 reshape.171
  94.8 4.4 %multiply_reduce_fusion = (f32[4096]{0:T(1024)S(1)}, f32[4096]{0:T(1024)S(1)}, f32[4096]{0:T(1024)S(1)}, f32[4096]{0:T(1024)S(1)}, f32[4096]{0:T(1024)S(1)}, /*index=5*/f32[4096]{0:T(1024)S(1)}) fusion(f32[25,3,4096]{2,1,0:T(4,128)} %reshape.171), kind=kLoop, calls=%fused_computation.56 | loop fusion | flops 1204224 | bytes 1327104 | tf_op jit(solution)/shard_map/reduce_sum | solution.py:30
  99.6 3.6 %collective-permute-start.7 = (f32[7,32,64]{2,0,1:T(8,128)S(1)}, f32[7,32,64]{2,0,1:T(8,128)S(1)}, u32[]{:S(2)}, u32[]{:S(2)}) collective-permute-start(f32[7,32,64]{2,0,1:T(8,128)S(1)} %get-tuple-element.43), channel_id=1, source_target_pairs={{0,1},{1,0},{2,3},{3,2},{4,5},{5,4},{6,7},{7,6},{8,9},{9,8},{10,11... | collective-permute-start | bytes 172040 | tf_op jit(solution)/shard_map/ppermute | solution.py:14
  104.0 17.8 %all-to-all-start = ((f32[1,128,1]{2,0,1:T(1,128)}), f32[1,128,1]{2,0,1:T(1,128)S(1)}, u32[]{:S(2)}, u32[]{:S(2)}) async-start(f32[1,128,1]{2,0,1:T(1,128)} %copy.49), calls=%async_computation | async-start | bytes 131072 | tf_op jit(solution)/shard_map/all_to_all | solution.py:143
  125.3 10.8 %all-to-all-done = f32[1,128,1]{2,0,1:T(1,128)S(1)} async-done(((f32[1,128,1]{2,0,1:T(1,128)}), f32[1,128,1]{2,0,1:T(1,128)S(1)}, u32[]{:S(2)}, u32[]{:S(2)}) %all-to-all-start) | async-done | bytes 544 | tf_op jit(solution)/shard_map/all_to_all | solution.py:143
  136.1 6.2 %all-to-all-start.3 = ((f32[128,1,448]{2,1,0:T(1,128)}), f32[128,1,448]{2,1,0:T(1,128)S(1)}, u32[]{:S(2)}, u32[]{:S(2)}) async-start(f32[128,1,448]{2,1,0:T(1,128)} %reshape.403), calls=%async_computation.3 | async-start | bytes 524288 | tf_op jit(solution)/shard_map/all_to_all | solution.py:142
  143.2 2.2 collective-permute-start.1
  146.4 12.9 %collective-permute-done.1 = bf16[100,32,64]{0,2,1:T(8,128)(2,1)S(1)} collective-permute-done((bf16[100,32,64]{0,2,1:T(8,128)(2,1)}, bf16[100,32,64]{0,2,1:T(8,128)(2,1)S(1)}, u32[]{:S(2)}, u32[]{:S(2)}) %collective-permute-start.1) | collective-permute-done | bytes 409632 | tf_op jit(solution)/shard_map/ppermute | solution.py:14
  159.3 2.2 gather_fusion.6
  161.5 3.3 %fusion.4 = bf16[100,128,64]{0,2,1:T(8,128)(2,1)} fusion(bf16[128,100,64]{1,2,0:T(8,128)(2,1)} %gather_fusion.6, bf16[128,100,64]{1,2,0:T(8,128)(2,1)S(1)} %gather_fusion.5, pred[128]{0:T(512)(128)(4,1)S(1)} %compare_and_fusion.9, pred[128]{0:T(512)(128)(4,1)S(1)} %copy-done.7, pred[128]{0:T(512)(128)(4,1)S(1)} %copy-done.6, pred[128]{0:T(512)(128)(4,1)S(1)} %fusion.36), kind=kLoop, calls=%fused_computation.30 | loop fusion | flops 3276800 | bytes 4915712 | tf_op jit(solution)/shard_map/jit(_where)/select_n | solution.py:124
  164.9 16.0 %all-to-all-start.1 = ((bf16[100,128,64]{0,2,1:T(8,128)(2,1)}), bf16[100,128,64]{0,2,1:T(8,128)(2,1)S(1)}, u32[]{:S(2)}, u32[]{:S(2)}) async-start(bf16[100,128,64]{0,2,1:T(8,128)(2,1)} %fusion.4), calls=%async_computation.1 | async-start | bytes 4194304 | tf_op jit(solution)/shard_map/all_to_all | solution.py:147
  180.9 2.4 convert_reduce_fusion
  183.3 2.5 sort.48
  186.6 2.5 sort.50
  193.4 2.2 collective-permute-start.8
  196.2 4.6 %collective-permute-done.8 = f32[7,32,64]{2,0,1:T(8,128)S(1)} collective-permute-done((f32[7,32,64]{2,0,1:T(8,128)S(1)}, f32[7,32,64]{2,0,1:T(8,128)S(1)}, u32[]{:S(2)}, u32[]{:S(2)}) %collective-permute-start.8) | collective-permute-done | bytes 57376 | tf_op jit(solution)/shard_map/ppermute | solution.py:14
  201.0 78.2 %all-to-all-done.1 = bf16[100,128,64]{0,2,1:T(8,128)(2,1)S(1)} async-done(((bf16[100,128,64]{0,2,1:T(8,128)(2,1)}), bf16[100,128,64]{0,2,1:T(8,128)(2,1)S(1)}, u32[]{:S(2)}, u32[]{:S(2)}) %all-to-all-start.1) | async-done | bytes 1638432 | tf_op jit(solution)/shard_map/all_to_all | solution.py:147
  279.9 2.2 collective-permute-start.2
  282.9 15.9 %all_to_all.29 = f32[7,32,128]{2,0,1:T(8,128)S(1)} all-to-all(f32[7,32,128]{2,0,1:T(8,128)S(1)} %select_bitcast_fusion.3), channel_id=1, replica_groups=mesh['wide'=128,'narrow'=4] {'narrow'}, dimensions={1} | all-to-all | bytes 229376 | tf_op jit(solution)/shard_map/all_to_all | solution.py:177
  304.1 3.5 %all-to-all-start.2 = ((bf16[100,32,128]{2,0,1:T(8,128)(2,1)}), bf16[100,32,128]{2,0,1:T(8,128)(2,1)S(1)}, u32[]{:S(2)}, u32[]{:S(2)}) async-start(bf16[100,32,128]{2,0,1:T(8,128)(2,1)} %select_bitcast_fusion), calls=%async_computation.2 | async-start | bytes 1703936 | tf_op jit(solution)/shard_map/all_to_all | solution.py:176
  308.2 12.8 %all-to-all-done.2 = bf16[100,32,128]{2,0,1:T(8,128)(2,1)S(1)} async-done(((bf16[100,32,128]{2,0,1:T(8,128)(2,1)}), bf16[100,32,128]{2,0,1:T(8,128)(2,1)S(1)}, u32[]{:S(2)}, u32[]{:S(2)}) %all-to-all-start.2) | async-done | bytes 819232 | tf_op jit(solution)/shard_map/all_to_all | solution.py:176
  (141 shorter events, 35.1 us)
Async XLA Ops:
  3.3 18.3 %copy-start.12 = (s32[32]{0:T(128)S(1)}, s32[32]{0:T(128)}, u32[]{:S(2)}) copy-start(s32[32]{0:T(128)} %param.24) | copy-start | bytes 388
  3.3 20.7 %copy-start.4 = (s32[4,4096]{1,0:T(4,128)S(1)}, s32[4,4096]{1,0:T(4,128)}, u32[]{:S(2)}) copy-start(s32[4,4096]{1,0:T(4,128)} %param.21) | copy-start | bytes 196612
  3.3 21.6 %copy-start.2 = (bf16[100,4096]{1,0:T(8,128)(2,1)S(1)}, bf16[100,4096]{1,0:T(8,128)(2,1)}, u32[]{:S(2)}) copy-start(bf16[100,4096]{1,0:T(8,128)(2,1)} %param.20) | copy-start | bytes 2457604
  3.3 21.6 %copy-start.3 = (bf16[5,75,100]{2,1,0:T(8,128)(2,1)S(1)}, bf16[5,75,100]{2,1,0:T(8,128)(2,1)}, u32[]{:S(2)}) copy-start(bf16[5,75,100]{2,1,0:T(8,128)(2,1)} %param.23) | copy-start | bytes 225004
  4.7 21.7 %copy-start.13 = (s32[32]{0:T(128)S(1)}, s32[32]{0:T(128)}, u32[]{:S(2)}) copy-start(s32[32]{0:T(128)} %param.25) | copy-start | bytes 388
  4.7 25.6 %collective-permute-start.3 = (bf16[100,2,128]{2,0,1:T(8,128)(2,1)S(1)}, bf16[100,2,128]{2,0,1:T(8,128)(2,1)S(1)}, u32[]{:S(2)}, u32[]{:S(2)}) collective-permute-start(bf16[100,2,128]{2,0,1:T(8,128)(2,1)S(1)} %select_bitcast_fusion.7), channel_id=1, source_target_pairs={{0,4},{4,8},{8,12},{12,16},{16,20},{20,24},{24,28},{28,32},{32,36}... | collective-permute-start | bytes 153608 | tf_op jit(solution)/shard_map/ppermute | solution.py:10
  7.4 22.8 %collective-permute-start.4 = (bf16[100,2,128]{2,0,1:T(8,128)(2,1)S(1)}, bf16[100,2,128]{2,0,1:T(8,128)(2,1)S(1)}, u32[]{:S(2)}, u32[]{:S(2)}) collective-permute-start(bf16[100,2,128]{2,0,1:T(8,128)(2,1)S(1)} %select_bitcast_fusion.6), channel_id=1, source_target_pairs={{0,508},{4,0},{8,4},{12,8},{16,12},{20,16},{24,20},{28,24},{32,28}... | collective-permute-start | bytes 153608 | tf_op jit(solution)/shard_map/ppermute | solution.py:10
  13.9 16.4 %collective-permute-start.5 = (bf16[100,2,128]{2,0,1:T(8,128)(2,1)S(1)}, bf16[100,2,128]{2,0,1:T(8,128)(2,1)S(1)}, u32[]{:S(2)}, u32[]{:S(2)}) collective-permute-start(bf16[100,2,128]{2,0,1:T(8,128)(2,1)S(1)} %select_bitcast_fusion.5), channel_id=1, source_target_pairs={{0,1},{1,2},{2,3},{3,0},{4,5},{5,6},{6,7},{7,4},{8,9},{9,10},{10,1... | collective-permute-start | bytes 153608 | tf_op jit(solution)/shard_map/ppermute | solution.py:10
  17.9 12.3 %collective-permute-start.6 = (bf16[100,2,128]{2,0,1:T(8,128)(2,1)S(1)}, bf16[100,2,128]{2,0,1:T(8,128)(2,1)S(1)}, u32[]{:S(2)}, u32[]{:S(2)}) collective-permute-start(bf16[100,2,128]{2,0,1:T(8,128)(2,1)S(1)} %select_bitcast_fusion.4), channel_id=1, source_target_pairs={{0,3},{1,0},{2,1},{3,2},{4,7},{5,4},{6,5},{7,6},{8,11},{9,8},{10,9... | collective-permute-start | bytes 153608 | tf_op jit(solution)/shard_map/ppermute | solution.py:10
  21.8 6.4 %collective-permute-start = (f32[2,32]{1,0:T(2,128)S(1)}, f32[2,32]{1,0:T(2,128)S(1)}, u32[]{:S(2)}, u32[]{:S(2)}) collective-permute-start(f32[2,32]{1,0:T(2,128)S(1)} %add_convert_fusion), channel_id=1, source_target_pairs={{0,1},{1,0},{2,3},{3,2},{4,5},{5,4},{6,7},{7,6},{8,9},{9,8},{10,11... | collective-permute-start | bytes 776 | tf_op jit(solution)/shard_map/ppermute | solution.py:14
  28.4 2.4 copy-start.10
  28.4 2.3 copy-start.5
  87.6 2.6 copy-start.1
  90.1 1.2 copy-start
  93.0 6.1 %copy-start.9 = (f32[32]{0:T(128)S(1)}, f32[32]{0:T(128)}, u32[]{:S(2)}) copy-start(f32[32]{0:T(128)} %convert_element_type.36) | copy-start | bytes 388
  94.7 8.5 %copy-start.11 = (s32[128]{0:T(128)S(1)}, s32[128]{0:T(128)}, u32[]{:S(2)}) copy-start(s32[128]{0:T(128)} %copy-done.10) | copy-start | bytes 1540
  94.8 8.5 %copy-start.8 = (f32[1,128,1]{1,2,0:T(1,128)S(1)}, f32[1,128,1]{1,2,0:T(1,128)}, u32[]{:S(2)}) copy-start(f32[1,128,1]{1,2,0:T(1,128)} %convert_bitcast_fusion) | copy-start | bytes 1540
  99.1 24.2 %copy-start.6 = (pred[128]{0:T(512)(128)(4,1)S(1)}, pred[128]{0:T(512)(128)(4,1)}, u32[]{:S(2)}) copy-start(pred[128]{0:T(512)(128)(4,1)} %copy-done.5) | copy-start | bytes 388
  99.1 24.2 %copy-start.7 = (pred[128]{0:T(512)(128)(4,1)S(1)}, pred[128]{0:T(512)(128)(4,1)}, u32[]{:S(2)}) copy-start(pred[128]{0:T(512)(128)(4,1)} %compare_and_fusion.10) | copy-start | bytes 388
  99.6 23.0 %collective-permute-start.7 = (f32[7,32,64]{2,0,1:T(8,128)S(1)}, f32[7,32,64]{2,0,1:T(8,128)S(1)}, u32[]{:S(2)}, u32[]{:S(2)}) collective-permute-start(f32[7,32,64]{2,0,1:T(8,128)S(1)} %get-tuple-element.43), channel_id=1, source_target_pairs={{0,1},{1,0},{2,3},{3,2},{4,5},{5,4},{6,7},{7,6},{8,9},{9,8},{10,11... | collective-permute-start | bytes 172040 | tf_op jit(solution)/shard_map/ppermute | solution.py:14
  104.0 32.1 %all-to-all-start = ((f32[1,128,1]{2,0,1:T(1,128)}), f32[1,128,1]{2,0,1:T(1,128)S(1)}, u32[]{:S(2)}, u32[]{:S(2)}) async-start(f32[1,128,1]{2,0,1:T(1,128)} %copy.49), calls=%async_computation | async-start | bytes 131072 | tf_op jit(solution)/shard_map/all_to_all | solution.py:143
  136.1 28.8 %all-to-all-start.3 = ((f32[128,1,448]{2,1,0:T(1,128)}), f32[128,1,448]{2,1,0:T(1,128)S(1)}, u32[]{:S(2)}, u32[]{:S(2)}) async-start(f32[128,1,448]{2,1,0:T(1,128)} %reshape.403), calls=%async_computation.3 | async-start | bytes 524288 | tf_op jit(solution)/shard_map/all_to_all | solution.py:142
  143.2 16.1 %collective-permute-start.1 = (bf16[100,32,64]{0,2,1:T(8,128)(2,1)}, bf16[100,32,64]{0,2,1:T(8,128)(2,1)S(1)}, u32[]{:S(2)}, u32[]{:S(2)}) collective-permute-start(bf16[100,32,64]{0,2,1:T(8,128)(2,1)} %get-tuple-element.39), channel_id=1, source_target_pairs={{0,1},{1,0},{2,3},{3,2},{4,5},{5,4},{6,7},{7,6},{8,9},{9,8},{10,11... | collective-permute-start | bytes 1228808 | tf_op jit(solution)/shard_map/ppermute | solution.py:14
  164.9 114.2 %all-to-all-start.1 = ((bf16[100,128,64]{0,2,1:T(8,128)(2,1)}), bf16[100,128,64]{0,2,1:T(8,128)(2,1)S(1)}, u32[]{:S(2)}, u32[]{:S(2)}) async-start(bf16[100,128,64]{0,2,1:T(8,128)(2,1)} %fusion.4), calls=%async_computation.1 | async-start | bytes 4194304 | tf_op jit(solution)/shard_map/all_to_all | solution.py:147
  193.4 7.4 %collective-permute-start.8 = (f32[7,32,64]{2,0,1:T(8,128)S(1)}, f32[7,32,64]{2,0,1:T(8,128)S(1)}, u32[]{:S(2)}, u32[]{:S(2)}) collective-permute-start(f32[7,32,64]{2,0,1:T(8,128)S(1)} %select_bitcast_fusion.2), channel_id=1, source_target_pairs={{0,1},{1,0},{2,3},{3,2},{4,5},{5,4},{6,7},{7,6},{8,9},{9,8},{10,11... | collective-permute-start | bytes 172040 | tf_op jit(solution)/shard_map/ppermute | solution.py:14
  279.9 20.2 %collective-permute-start.2 = (bf16[100,32,64]{0,2,1:T(8,128)(2,1)S(1)}, bf16[100,32,64]{0,2,1:T(8,128)(2,1)}, u32[]{:S(2)}, u32[]{:S(2)}) collective-permute-start(bf16[100,32,64]{0,2,1:T(8,128)(2,1)S(1)} %select_bitcast_fusion.1), channel_id=1, source_target_pairs={{0,1},{1,0},{2,3},{3,2},{4,5},{5,4},{6,7},{7,6},{8,9},{9,8},{10,11... | collective-permute-start | bytes 1228808 | tf_op jit(solution)/shard_map/ppermute | solution.py:14
  304.1 17.0 %all-to-all-start.2 = ((bf16[100,32,128]{2,0,1:T(8,128)(2,1)}), bf16[100,32,128]{2,0,1:T(8,128)(2,1)S(1)}, u32[]{:S(2)}, u32[]{:S(2)}) async-start(bf16[100,32,128]{2,0,1:T(8,128)(2,1)} %select_bitcast_fusion), calls=%async_computation.2 | async-start | bytes 1703936 | tf_op jit(solution)/shard_map/all_to_all | solution.py:176
where the time goes:
time: 323 us
  waiting for transfers between devices  120 us (37%)
  local copies, waits for them, and re-layouts  83.2 us (26%)
  starting transfers between devices  70.8 us (22%)
  other arithmetic  25.1 us (8%)
  blocking collectives  15.9 us (5%)
  matrix products  6.45 us (2%)
    all_to_all x1, waiting for transfers between devices, per_device(): lax.all_to_all(joined_coeffs, 'wide', split_axis=1, concat_axis=1, tiled=...  78.2 us
    gather x4, local copies, waits for them, and re-layouts, per_device(): gathered = jnp.take(extended, neighbours[face_index], axis=1)  56.8 us
    all_to_all x1, starting transfers between devices, per_device(): lax.all_to_all(pair_tags.astype(jnp.float32)[None, :], 'wide', split_axis...  17.8 us
    ppermute x5, waiting for transfers between devices, swapped(): lax.ppermute(value, axis, [(i, i ^ 1 << apart) for i in range(lax.axis_si...  17.6 us
    all_to_all x1, starting transfers between devices, per_device(): lax.all_to_all(joined_coeffs, 'wide', split_axis=1, concat_axis=1, tiled=...  16 us
    all_to_all x1, blocking collectives, per_device(): lax.all_to_all(relayed_stats, 'narrow', split_axis=1, concat_axis=1, tile...  15.9 us
    ppermute x4, starting transfers between devices, passed_along(): return lax.ppermute(value, axis, pairs)  14.8 us
    all_to_all x1, waiting for transfers between devices, per_device(): lax.all_to_all(relayed_coeffs, 'narrow', split_axis=1, concat_axis=1, til...  12.8 us
  transfers between devices with their start and end apart: 13, of which 6 were waited for; matrix products, arithmetic and copies ran while one was open for 11% of the time, Pallas kernels for 0%

commit v1 on v0

--- a/solution.py
+++ b/solution.py
@@ -174,7 +174,12 @@
     relayed_coeffs = jnp.take(whole_coeffs, through, axis=1)
     relayed_stats = jnp.take(whole_stats, through, axis=1)
     new_coeffs = lax.all_to_all(relayed_coeffs, "narrow", split_axis=1, concat_axis=1, tiled=True)
-    new_stats = lax.all_to_all(relayed_stats, "narrow", split_axis=1, concat_axis=1, tiled=True)
+    new_stats = jnp.concatenate(
+        lax.all_to_all(
+            jnp.stack(jnp.split(relayed_stats, lax.axis_size("narrow"), axis=1)), "narrow", 0, 0
+        ),
+        axis=1,
+    )
     flat_stats = new_stats.reshape(7, elem_count)
     return (new_coeffs.reshape(coeff_count, elem_count), flat_stats[:6], flat_stats[6])
 

time: 323 us -> 320 us (level)
  blocking collectives: 15.9 us -> 0 us
  waiting for transfers between devices: 120 us -> 127 us
  starting transfers between devices: 70.8 us -> 74.7 us
    all_to_all x1 -> x0, blocking collectives: 15.9 us -> none  [per_device(): lax.all_to_all(relayed_stats, 'narrow', split_axis=1, concat_axis=1, tile...]
    ppermute x5, waiting for transfers between devices: 17.6 us -> 26.6 us  [swapped(): lax.ppermute(value, axis, [(i, i ^ 1 << apart) for i in range(lax.axis_si...]
    all_to_all x0 -> x1, starting transfers between devices: none -> 3.99 us  [per_device(): lax.all_to_all(jnp.stack(jnp.split(relayed_stats, lax.axis_size('narrow')...]
  transfers between devices with their start and end apart: 13 -> 14, of which waited for: 6 -> 7; matrix products, arithmetic and copies ran while one was open for 11% -> 13% of each run, Pallas kernels for 0% -> 0%
where the time goes in v1:
time: 320 us; the launch traced here: 319 us
  waiting for transfers between devices  127 us (40%)
  local copies, waits for them, and re-layouts  83.9 us (26%)
  starting transfers between devices  74.7 us (23%)
  other arithmetic  25.1 us (8%)
  matrix products  6.45 us (2%)
    all_to_all x1, waiting for transfers between devices, per_device(): lax.all_to_all(joined_coeffs, 'wide', split_axis=1, concat_axis=1, tiled=...  77.5 us
    gather x4, local copies, waits for them, and re-layouts, per_device(): gathered = jnp.take(extended, neighbours[face_index], axis=1)  56.8 us
    ppermute x5, waiting for transfers between devices, swapped(): lax.ppermute(value, axis, [(i, i ^ 1 << apart) for i in range(lax.axis_si...  26.6 us
    all_to_all x1, starting transfers between devices, per_device(): lax.all_to_all(pair_tags.astype(jnp.float32)[None, :], 'wide', split_axis...  17.8 us
    all_to_all x1, starting transfers between devices, per_device(): lax.all_to_all(joined_coeffs, 'wide', split_axis=1, concat_axis=1, tiled=...  16 us
    ppermute x4, starting transfers between devices, passed_along(): return lax.ppermute(value, axis, pairs)  14.8 us
    ppermute x5, starting transfers between devices, swapped(): lax.ppermute(value, axis, [(i, i ^ 1 << apart) for i in range(lax.axis_si...  12.4 us
    all_to_all x1, waiting for transfers between devices, per_device(): lax.all_to_all(relayed_coeffs, 'narrow', split_axis=1, concat_axis=1, til...  12.3 us
  transfers between devices with their start and end apart: 14, of which 7 were waited for; matrix products, arithmetic and copies ran while one was open for 13% of the time, Pallas kernels for 0%

profile of v1, /device:TPU:32, one launch (start us, length us, event | category | flops | bytes accessed | tf_op | source)
XLA Modules:
  0.0 319.1 jit_solution(6815072162431226506)
XLA Ops:
  4.7 2.0 collective-permute-start.3
  7.4 5.7 %collective-permute-start.4 = (bf16[100,2,128]{2,0,1:T(8,128)(2,1)S(1)}, bf16[100,2,128]{2,0,1:T(8,128)(2,1)S(1)}, u32[]{:S(2)}, u32[]{:S(2)}) collective-permute-start(bf16[100,2,128]{2,0,1:T(8,128)(2,1)S(1)} %select_bitcast_fusion.6), channel_id=1, source_target_pairs={{0,508},{4,0},{8,4},{12,8},{16,12},{20,16},{24,20},{28,24},{32,28}... | collective-permute-start | bytes 153608 | tf_op jit(solution)/shard_map/ppermute | solution.py:10
  13.9 3.4 %collective-permute-start.5 = (bf16[100,2,128]{2,0,1:T(8,128)(2,1)S(1)}, bf16[100,2,128]{2,0,1:T(8,128)(2,1)S(1)}, u32[]{:S(2)}, u32[]{:S(2)}) collective-permute-start(bf16[100,2,128]{2,0,1:T(8,128)(2,1)S(1)} %select_bitcast_fusion.5), channel_id=1, source_target_pairs={{0,1},{1,2},{2,3},{3,0},{4,5},{5,6},{6,7},{7,4},{8,9},{9,10},{10,1... | collective-permute-start | bytes 153608 | tf_op jit(solution)/shard_map/ppermute | solution.py:10
  17.9 3.6 %collective-permute-start.6 = (bf16[100,2,128]{2,0,1:T(8,128)(2,1)S(1)}, bf16[100,2,128]{2,0,1:T(8,128)(2,1)S(1)}, u32[]{:S(2)}, u32[]{:S(2)}) collective-permute-start(bf16[100,2,128]{2,0,1:T(8,128)(2,1)S(1)} %select_bitcast_fusion.4), channel_id=1, source_target_pairs={{0,3},{1,0},{2,1},{3,2},{4,7},{5,4},{6,5},{7,6},{8,11},{9,8},{10,9... | collective-permute-start | bytes 153608 | tf_op jit(solution)/shard_map/ppermute | solution.py:10
  21.8 2.2 collective-permute-start
  30.8 14.9 %gather_fusion.13 = bf16[4096,100]{1,0:T(8,128)(2,1)} fusion(bf16[100,5120]{0,1:T(8,128)(2,1)S(1)} %pad_maximum_fusion, s32[4096]{0:T(1024)S(1)} %fusion.38), kind=kCustom, calls=%fused_computation.4.clone | custom fusion | bytes 1654784 | tf_op jit(solution)/shard_map/jit(_take)/gather | solution.py:86
  45.7 14.9 %gather_fusion.14 = bf16[4096,100]{1,0:T(8,128)(2,1)} fusion(bf16[100,5120]{0,1:T(8,128)(2,1)S(1)} %pad_maximum_fusion, s32[4096]{0:T(1024)S(1)} %fusion.39), kind=kCustom, calls=%fused_computation.13.clone | custom fusion | bytes 1654784 | tf_op jit(solution)/shard_map/jit(_take)/gather | solution.py:86
  60.6 14.9 %gather_fusion.15 = bf16[4096,100]{1,0:T(8,128)(2,1)} fusion(bf16[100,5120]{0,1:T(8,128)(2,1)S(1)} %pad_maximum_fusion, s32[4096]{0:T(1024)S(1)} %fusion.40), kind=kCustom, calls=%fused_computation.14.clone | custom fusion | bytes 1654784 | tf_op jit(solution)/shard_map/jit(_take)/gather | solution.py:86
  75.4 12.1 %gather_fusion.16 = bf16[4096,100]{1,0:T(8,128)(2,1)S(1)} fusion(bf16[100,5120]{0,1:T(8,128)(2,1)S(1)} %pad_maximum_fusion, s32[4096]{0:T(1024)S(1)} %fusion.41), kind=kCustom, calls=%fused_computation.15.clone | custom fusion | bytes 1654784 | tf_op jit(solution)/shard_map/jit(_take)/gather | solution.py:86
  87.6 2.5 fusion.3
  93.0 1.7 reshape.173
  94.8 4.4 %multiply_reduce_fusion = (f32[4096]{0:T(1024)S(1)}, f32[4096]{0:T(1024)S(1)}, f32[4096]{0:T(1024)S(1)}, f32[4096]{0:T(1024)S(1)}, f32[4096]{0:T(1024)S(1)}, /*index=5*/f32[4096]{0:T(1024)S(1)}) fusion(f32[25,3,4096]{2,1,0:T(4,128)} %reshape.173), kind=kLoop, calls=%fused_computation.56 | loop fusion | flops 1204224 | bytes 1327104 | tf_op jit(solution)/shard_map/reduce_sum | solution.py:30
  99.6 3.6 %collective-permute-start.7 = (f32[7,32,64]{2,0,1:T(8,128)S(1)}, f32[7,32,64]{2,0,1:T(8,128)S(1)}, u32[]{:S(2)}, u32[]{:S(2)}) collective-permute-start(f32[7,32,64]{2,0,1:T(8,128)S(1)} %get-tuple-element.43), channel_id=1, source_target_pairs={{0,1},{1,0},{2,3},{3,2},{4,5},{5,4},{6,7},{7,6},{8,9},{9,8},{10,11... | collective-permute-start | bytes 172040 | tf_op jit(solution)/shard_map/ppermute | solution.py:14
  104.0 17.8 %all-to-all-start = ((f32[1,128,1]{2,0,1:T(1,128)}), f32[1,128,1]{2,0,1:T(1,128)S(1)}, u32[]{:S(2)}, u32[]{:S(2)}) async-start(f32[1,128,1]{2,0,1:T(1,128)} %copy.55), calls=%async_computation | async-start | bytes 131072 | tf_op jit(solution)/shard_map/all_to_all | solution.py:143
  125.3 10.8 %all-to-all-done = f32[1,128,1]{2,0,1:T(1,128)S(1)} async-done(((f32[1,128,1]{2,0,1:T(1,128)}), f32[1,128,1]{2,0,1:T(1,128)S(1)}, u32[]{:S(2)}, u32[]{:S(2)}) %all-to-all-start) | async-done | bytes 544 | tf_op jit(solution)/shard_map/all_to_all | solution.py:143
  136.1 6.2 %all-to-all-start.3 = ((f32[128,1,448]{2,1,0:T(1,128)}), f32[128,1,448]{2,1,0:T(1,128)S(1)}, u32[]{:S(2)}, u32[]{:S(2)}) async-start(f32[128,1,448]{2,1,0:T(1,128)} %reshape.406), calls=%async_computation.3 | async-start | bytes 524288 | tf_op jit(solution)/shard_map/all_to_all | solution.py:142
  143.2 2.2 collective-permute-start.1
  146.4 12.9 %collective-permute-done.1 = bf16[100,32,64]{0,2,1:T(8,128)(2,1)S(1)} collective-permute-done((bf16[100,32,64]{0,2,1:T(8,128)(2,1)}, bf16[100,32,64]{0,2,1:T(8,128)(2,1)S(1)}, u32[]{:S(2)}, u32[]{:S(2)}) %collective-permute-start.1) | collective-permute-done | bytes 409632 | tf_op jit(solution)/shard_map/ppermute | solution.py:14
  159.3 2.2 gather_fusion.6
  161.5 3.3 %fusion.4 = bf16[100,128,64]{0,2,1:T(8,128)(2,1)} fusion(bf16[128,100,64]{1,2,0:T(8,128)(2,1)} %gather_fusion.6, bf16[128,100,64]{1,2,0:T(8,128)(2,1)S(1)} %gather_fusion.5, pred[128]{0:T(512)(128)(4,1)S(1)} %compare_and_fusion.9, pred[128]{0:T(512)(128)(4,1)S(1)} %copy-done.7, pred[128]{0:T(512)(128)(4,1)S(1)} %copy-done.6, pred[128]{0:T(512)(128)(4,1)S(1)} %fusion.36), kind=kLoop, calls=%fused_computation.30 | loop fusion | flops 3276800 | bytes 4915712 | tf_op jit(solution)/shard_map/jit(_where)/select_n | solution.py:124
  164.9 16.0 %all-to-all-start.1 = ((bf16[100,128,64]{0,2,1:T(8,128)(2,1)}), bf16[100,128,64]{0,2,1:T(8,128)(2,1)S(1)}, u32[]{:S(2)}, u32[]{:S(2)}) async-start(bf16[100,128,64]{0,2,1:T(8,128)(2,1)} %fusion.4), calls=%async_computation.1 | async-start | bytes 4194304 | tf_op jit(solution)/shard_map/all_to_all | solution.py:147
  180.9 2.4 convert_reduce_fusion
  183.3 2.5 sort.48
  186.6 2.5 sort.50
  193.4 2.2 collective-permute-start.8
  196.2 4.6 %collective-permute-done.8 = f32[7,32,64]{2,0,1:T(8,128)S(1)} collective-permute-done((f32[7,32,64]{2,0,1:T(8,128)S(1)}, f32[7,32,64]{2,0,1:T(8,128)S(1)}, u32[]{:S(2)}, u32[]{:S(2)}) %collective-permute-start.8) | collective-permute-done | bytes 57376 | tf_op jit(solution)/shard_map/ppermute | solution.py:14
  201.7 77.5 %all-to-all-done.1 = bf16[100,128,64]{0,2,1:T(8,128)(2,1)S(1)} async-done(((bf16[100,128,64]{0,2,1:T(8,128)(2,1)}), bf16[100,128,64]{0,2,1:T(8,128)(2,1)S(1)}, u32[]{:S(2)}, u32[]{:S(2)}) %all-to-all-start.1) | async-done | bytes 1638432 | tf_op jit(solution)/shard_map/all_to_all | solution.py:147
  279.9 2.2 collective-permute-start.2
  282.9 4.0 %all-to-all-start.4 = ((f32[4,7,8,128]{3,2,1,0:T(8,128)}), f32[4,7,8,128]{3,2,1,0:T(8,128)S(1)}, u32[]{:S(2)}, u32[]{:S(2)}) async-start(f32[4,7,8,128]{3,2,1,0:T(8,128)} %copy.66), calls=%async_computation.4 | async-start | bytes 229376 | tf_op jit(solution)/shard_map/all_to_all | solution.py:178
  287.6 9.0 %collective-permute-done.2 = bf16[100,32,64]{0,2,1:T(8,128)(2,1)} collective-permute-done((bf16[100,32,64]{0,2,1:T(8,128)(2,1)S(1)}, bf16[100,32,64]{0,2,1:T(8,128)(2,1)}, u32[]{:S(2)}, u32[]{:S(2)}) %collective-permute-start.2) | collective-permute-done | bytes 409632 | tf_op jit(solution)/shard_map/ppermute | solution.py:14
  300.5 3.5 %all-to-all-start.2 = ((bf16[100,32,128]{2,0,1:T(8,128)(2,1)}), bf16[100,32,128]{2,0,1:T(8,128)(2,1)S(1)}, u32[]{:S(2)}, u32[]{:S(2)}) async-start(bf16[100,32,128]{2,0,1:T(8,128)(2,1)} %select_bitcast_fusion), calls=%async_computation.2 | async-start | bytes 1703936 | tf_op jit(solution)/shard_map/all_to_all | solution.py:176
  305.4 12.3 %all-to-all-done.2 = bf16[100,32,128]{2,0,1:T(8,128)(2,1)S(1)} async-done(((bf16[100,32,128]{2,0,1:T(8,128)(2,1)}), bf16[100,32,128]{2,0,1:T(8,128)(2,1)S(1)}, u32[]{:S(2)}, u32[]{:S(2)}) %all-to-all-start.2) | async-done | bytes 819232 | tf_op jit(solution)/shard_map/all_to_all | solution.py:176
  (146 shorter events, 37.4 us)
Async XLA Ops:
  3.3 18.3 %copy-start.12 = (s32[32]{0:T(128)S(1)}, s32[32]{0:T(128)}, u32[]{:S(2)}) copy-start(s32[32]{0:T(128)} %param.24) | copy-start | bytes 388
  3.3 20.7 %copy-start.4 = (s32[4,4096]{1,0:T(4,128)S(1)}, s32[4,4096]{1,0:T(4,128)}, u32[]{:S(2)}) copy-start(s32[4,4096]{1,0:T(4,128)} %param.21) | copy-start | bytes 196612
  3.3 21.6 %copy-start.2 = (bf16[100,4096]{1,0:T(8,128)(2,1)S(1)}, bf16[100,4096]{1,0:T(8,128)(2,1)}, u32[]{:S(2)}) copy-start(bf16[100,4096]{1,0:T(8,128)(2,1)} %param.20) | copy-start | bytes 2457604
  3.3 21.6 %copy-start.3 = (bf16[5,75,100]{2,1,0:T(8,128)(2,1)S(1)}, bf16[5,75,100]{2,1,0:T(8,128)(2,1)}, u32[]{:S(2)}) copy-start(bf16[5,75,100]{2,1,0:T(8,128)(2,1)} %param.23) | copy-start | bytes 225004
  4.7 21.7 %copy-start.13 = (s32[32]{0:T(128)S(1)}, s32[32]{0:T(128)}, u32[]{:S(2)}) copy-start(s32[32]{0:T(128)} %param.25) | copy-start | bytes 388
  4.7 25.6 %collective-permute-start.3 = (bf16[100,2,128]{2,0,1:T(8,128)(2,1)S(1)}, bf16[100,2,128]{2,0,1:T(8,128)(2,1)S(1)}, u32[]{:S(2)}, u32[]{:S(2)}) collective-permute-start(bf16[100,2,128]{2,0,1:T(8,128)(2,1)S(1)} %select_bitcast_fusion.7), channel_id=1, source_target_pairs={{0,4},{4,8},{8,12},{12,16},{16,20},{20,24},{24,28},{28,32},{32,36}... | collective-permute-start | bytes 153608 | tf_op jit(solution)/shard_map/ppermute | solution.py:10
  7.4 22.8 %collective-permute-start.4 = (bf16[100,2,128]{2,0,1:T(8,128)(2,1)S(1)}, bf16[100,2,128]{2,0,1:T(8,128)(2,1)S(1)}, u32[]{:S(2)}, u32[]{:S(2)}) collective-permute-start(bf16[100,2,128]{2,0,1:T(8,128)(2,1)S(1)} %select_bitcast_fusion.6), channel_id=1, source_target_pairs={{0,508},{4,0},{8,4},{12,8},{16,12},{20,16},{24,20},{28,24},{32,28}... | collective-permute-start | bytes 153608 | tf_op jit(solution)/shard_map/ppermute | solution.py:10
  13.9 16.4 %collective-permute-start.5 = (bf16[100,2,128]{2,0,1:T(8,128)(2,1)S(1)}, bf16[100,2,128]{2,0,1:T(8,128)(2,1)S(1)}, u32[]{:S(2)}, u32[]{:S(2)}) collective-permute-start(bf16[100,2,128]{2,0,1:T(8,128)(2,1)S(1)} %select_bitcast_fusion.5), channel_id=1, source_target_pairs={{0,1},{1,2},{2,3},{3,0},{4,5},{5,6},{6,7},{7,4},{8,9},{9,10},{10,1... | collective-permute-start | bytes 153608 | tf_op jit(solution)/shard_map/ppermute | solution.py:10
  17.9 12.3 %collective-permute-start.6 = (bf16[100,2,128]{2,0,1:T(8,128)(2,1)S(1)}, bf16[100,2,128]{2,0,1:T(8,128)(2,1)S(1)}, u32[]{:S(2)}, u32[]{:S(2)}) collective-permute-start(bf16[100,2,128]{2,0,1:T(8,128)(2,1)S(1)} %select_bitcast_fusion.4), channel_id=1, source_target_pairs={{0,3},{1,0},{2,1},{3,2},{4,7},{5,4},{6,5},{7,6},{8,11},{9,8},{10,9... | collective-permute-start | bytes 153608 | tf_op jit(solution)/shard_map/ppermute | solution.py:10
  21.8 6.4 %collective-permute-start = (f32[2,32]{1,0:T(2,128)S(1)}, f32[2,32]{1,0:T(2,128)S(1)}, u32[]{:S(2)}, u32[]{:S(2)}) collective-permute-start(f32[2,32]{1,0:T(2,128)S(1)} %add_convert_fusion), channel_id=1, source_target_pairs={{0,1},{1,0},{2,3},{3,2},{4,5},{5,4},{6,7},{7,6},{8,9},{9,8},{10,11... | collective-permute-start | bytes 776 | tf_op jit(solution)/shard_map/ppermute | solution.py:14
  28.4 2.4 copy-start.10
  28.4 2.3 copy-start.5
  87.6 2.6 copy-start.1
  90.1 1.2 copy-start
  93.0 6.1 %copy-start.9 = (f32[32]{0:T(128)S(1)}, f32[32]{0:T(128)}, u32[]{:S(2)}) copy-start(f32[32]{0:T(128)} %convert_element_type.36) | copy-start | bytes 388
  94.7 8.5 %copy-start.11 = (s32[128]{0:T(128)S(1)}, s32[128]{0:T(128)}, u32[]{:S(2)}) copy-start(s32[128]{0:T(128)} %copy-done.10) | copy-start | bytes 1540
  94.8 8.5 %copy-start.8 = (f32[1,128,1]{1,2,0:T(1,128)S(1)}, f32[1,128,1]{1,2,0:T(1,128)}, u32[]{:S(2)}) copy-start(f32[1,128,1]{1,2,0:T(1,128)} %convert_bitcast_fusion) | copy-start | bytes 1540
  99.1 24.2 %copy-start.6 = (pred[128]{0:T(512)(128)(4,1)S(1)}, pred[128]{0:T(512)(128)(4,1)}, u32[]{:S(2)}) copy-start(pred[128]{0:T(512)(128)(4,1)} %copy-done.5) | copy-start | bytes 388
  99.1 24.2 %copy-start.7 = (pred[128]{0:T(512)(128)(4,1)S(1)}, pred[128]{0:T(512)(128)(4,1)}, u32[]{:S(2)}) copy-start(pred[128]{0:T(512)(128)(4,1)} %compare_and_fusion.10) | copy-start | bytes 388
  99.6 23.0 %collective-permute-start.7 = (f32[7,32,64]{2,0,1:T(8,128)S(1)}, f32[7,32,64]{2,0,1:T(8,128)S(1)}, u32[]{:S(2)}, u32[]{:S(2)}) collective-permute-start(f32[7,32,64]{2,0,1:T(8,128)S(1)} %get-tuple-element.43), channel_id=1, source_target_pairs={{0,1},{1,0},{2,3},{3,2},{4,5},{5,4},{6,7},{7,6},{8,9},{9,8},{10,11... | collective-permute-start | bytes 172040 | tf_op jit(solution)/shard_map/ppermute | solution.py:14
  104.0 32.1 %all-to-all-start = ((f32[1,128,1]{2,0,1:T(1,128)}), f32[1,128,1]{2,0,1:T(1,128)S(1)}, u32[]{:S(2)}, u32[]{:S(2)}) async-start(f32[1,128,1]{2,0,1:T(1,128)} %copy.55), calls=%async_computation | async-start | bytes 131072 | tf_op jit(solution)/shard_map/all_to_all | solution.py:143
  136.1 28.8 %all-to-all-start.3 = ((f32[128,1,448]{2,1,0:T(1,128)}), f32[128,1,448]{2,1,0:T(1,128)S(1)}, u32[]{:S(2)}, u32[]{:S(2)}) async-start(f32[128,1,448]{2,1,0:T(1,128)} %reshape.406), calls=%async_computation.3 | async-start | bytes 524288 | tf_op jit(solution)/shard_map/all_to_all | solution.py:142
  143.2 16.1 %collective-permute-start.1 = (bf16[100,32,64]{0,2,1:T(8,128)(2,1)}, bf16[100,32,64]{0,2,1:T(8,128)(2,1)S(1)}, u32[]{:S(2)}, u32[]{:S(2)}) collective-permute-start(bf16[100,32,64]{0,2,1:T(8,128)(2,1)} %get-tuple-element.39), channel_id=1, source_target_pairs={{0,1},{1,0},{2,3},{3,2},{4,5},{5,4},{6,7},{7,6},{8,9},{9,8},{10,11... | collective-permute-start | bytes 1228808 | tf_op jit(solution)/shard_map/ppermute | solution.py:14
  164.9 114.2 %all-to-all-start.1 = ((bf16[100,128,64]{0,2,1:T(8,128)(2,1)}), bf16[100,128,64]{0,2,1:T(8,128)(2,1)S(1)}, u32[]{:S(2)}, u32[]{:S(2)}) async-start(bf16[100,128,64]{0,2,1:T(8,128)(2,1)} %fusion.4), calls=%async_computation.1 | async-start | bytes 4194304 | tf_op jit(solution)/shard_map/all_to_all | solution.py:147
  193.4 7.4 %collective-permute-start.8 = (f32[7,32,64]{2,0,1:T(8,128)S(1)}, f32[7,32,64]{2,0,1:T(8,128)S(1)}, u32[]{:S(2)}, u32[]{:S(2)}) collective-permute-start(f32[7,32,64]{2,0,1:T(8,128)S(1)} %select_bitcast_fusion.2), channel_id=1, source_target_pairs={{0,1},{1,0},{2,3},{3,2},{4,5},{5,4},{6,7},{7,6},{8,9},{9,8},{10,11... | collective-permute-start | bytes 172040 | tf_op jit(solution)/shard_map/ppermute | solution.py:14
  279.9 16.7 %collective-permute-start.2 = (bf16[100,32,64]{0,2,1:T(8,128)(2,1)S(1)}, bf16[100,32,64]{0,2,1:T(8,128)(2,1)}, u32[]{:S(2)}, u32[]{:S(2)}) collective-permute-start(bf16[100,32,64]{0,2,1:T(8,128)(2,1)S(1)} %select_bitcast_fusion.1), channel_id=1, source_target_pairs={{0,1},{1,0},{2,3},{3,2},{4,5},{5,4},{6,7},{7,6},{8,9},{9,8},{10,11... | collective-permute-start | bytes 1228808 | tf_op jit(solution)/shard_map/ppermute | solution.py:14
  282.9 17.6 %all-to-all-start.4 = ((f32[4,7,8,128]{3,2,1,0:T(8,128)}), f32[4,7,8,128]{3,2,1,0:T(8,128)S(1)}, u32[]{:S(2)}, u32[]{:S(2)}) async-start(f32[4,7,8,128]{3,2,1,0:T(8,128)} %copy.66), calls=%async_computation.4 | async-start | bytes 229376 | tf_op jit(solution)/shard_map/all_to_all | solution.py:178
  300.5 17.2 %all-to-all-start.2 = ((bf16[100,32,128]{2,0,1:T(8,128)(2,1)}), bf16[100,32,128]{2,0,1:T(8,128)(2,1)S(1)}, u32[]{:S(2)}, u32[]{:S(2)}) async-start(bf16[100,32,128]{2,0,1:T(8,128)(2,1)} %select_bitcast_fusion), calls=%async_computation.2 | async-start | bytes 1703936 | tf_op jit(solution)/shard_map/all_to_all | solution.py:176
